TPU v7x, 128 devices: a whole 4x4x4 slice. The times are simulated.
128 devices in a mesh: group: 32 (over x_hi, z, y), blk: 4 (over x_lo, core).
Axes of the slice: x: 4 (x_hi: 2, x_lo: 2; x = x_hi * 2 + x_lo), y: 4, z: 4, core: 2. Of those that a mesh axis runs over, the one named last changes fastest.
Arguments:
- sources: bfloat16 [4, 1048576, 128], P(None, ('group', 'blk')), may hold values from -0.09375 to 0.09375
- positions: float32 [3, 1048576], P(None, ('group', 'blk')), may hold values from -1 to 1, as said below
- counts: int32 [128], P(('group', 'blk')), may hold values from 1024 to 8192, as said below
- offsets: int32 [2048, 4], P(('group', 'blk')), may hold values from 0 to 47, as said below
- observers: float32 [3, 512], P(None, 'blk'), may hold values from -1.35 to 1.35, as said below
Outputs:
- pressure: float32 [512, 128], P('blk', 'group')
Inputs may be any that keep to these rules, and one draw needn't show every extreme that they name: `counts`: each block's count is at least 1024, and some block is full, with exactly 8192 live faces. `offsets`: offsets take the value 0 and the value 48 - 1 somewhere in every draw. `positions`: every face centre lies on the surface of the cube from -1 to 1: some coordinate is -1 or 1. `observers`: each observer has some coordinate of magnitude 1.25 or more.
All inputs are finite; a program needn't handle non-finite values.
Results may differ from a plain program's by a relative error of at most 0.014.
Values may be sent and summed in bfloat16 or wider, within the bound.
No kernel may reach another device: no remote copies, remote signals or barrier semaphores. Data moves between devices by JAX's collectives and lax.ppermute only.
A program may use at most 128 MiB of HBM per device.

v0:
```python
import jax
import jax.numpy as jnp
from jax import lax
from jax.sharding import PartitionSpec as P

FSUB = 512


def make_channels(source_piece):
    loads = source_piece[1:4].astype(jnp.float32)
    padded = jnp.pad(loads, ((0, 0), (0, 0), (1, 1)))
    rate = (padded[:, :, 2:] - padded[:, :, :-2]).astype(jnp.bfloat16)
    return jnp.concatenate([source_piece, rate], 0)


def make_coeffs(face_pos, observer_pos, valid):
    diff = observer_pos[:, None, :] - face_pos[:, :, None]
    inv = lax.rsqrt(jnp.sum(diff * diff, 0))
    unit = diff * inv[None]
    coeffs = jnp.concatenate([inv[None], unit * (inv * inv)[None], unit * inv[None]], 0)
    return (coeffs * valid[None, :, None]).astype(jnp.bfloat16)


def delayed(signal, shifts):
    groups = shifts.shape[0]
    samples = signal.shape[1]
    blocks = signal.reshape(groups, signal.shape[0] // groups, samples)
    padded = jnp.concatenate([jnp.zeros_like(blocks), blocks], 2)

    def move(block, shift):
        return lax.dynamic_slice_in_dim(block, samples - shift, samples, 1)

    return jax.vmap(move)(padded, shifts).reshape(signal.shape)


def sub_term(source_piece, face_pos, observer_pos, valid, shifts):
    sub = source_piece.shape[1]
    chans = make_channels(source_piece).reshape(7 * sub, source_piece.shape[2])
    coeffs = make_coeffs(face_pos, observer_pos, valid).reshape(7 * sub, observer_pos.shape[1])
    signal = lax.dot_general(
        coeffs, chans, (((0,), (0,)), ((), ())), preferred_element_type=jnp.float32
    )
    return delayed(signal, shifts)


def block_signal(sources, positions, live, shift_table, observer_pos):
    nsub = sources.shape[1] // FSUB
    start_total = jnp.zeros((observer_pos.shape[1], sources.shape[2]), jnp.float32)

    def one_sub(index, acc):
        first = (index * FSUB).astype(jnp.int32)
        piece = lax.dynamic_slice_in_dim(sources, first, FSUB, 1)
        face_pos = lax.dynamic_slice_in_dim(positions, first, FSUB, 1)
        shifts = shift_table[index]
        valid = (first + jnp.arange(FSUB, dtype=jnp.int32) < live).astype(jnp.float32)
        return acc + sub_term(piece, face_pos, observer_pos, valid, shifts)

    return lax.fori_loop(0, nsub, one_sub, start_total)


def body(sources, positions, counts, offsets, observers):
    everyone = lax.all_gather(observers, "blk", axis=1, tiled=True)
    partial_all = block_signal(sources, positions, counts[0], offsets, everyone)
    summed = lax.psum_scatter(partial_all, "group", scatter_dimension=1, tiled=True)
    summed = lax.psum_scatter(summed, "blk", scatter_dimension=0, tiled=True)
    return summed * (1.0 / (4.0 * jnp.pi))


def solution(mesh):
    return jax.shard_map(
        body,
        mesh=mesh,
        in_specs=(
            P(None, ("group", "blk"), None),
            P(None, ("group", "blk")),
            P(("group", "blk")),
            P(("group", "blk"), None),
            P(None, "blk"),
        ),
        out_specs=P("blk", "group"),
        check_vma=False,
    )
```

profile of v0, /device:TPU:1, one launch (start us, length us, event | category | flops | bytes accessed | tf_op | source)
XLA Modules:
  0.0 761.6 jit_solution(5166264477792664920)
XLA Ops:
  6.5 6.5 all_gather.3
  13.8 367.6 %while.16 = (s32[]{:T(128)}, f32[512,128]{0,1:T(8,128)S(1)}, f32[3,512]{1,0:T(4,128)S(1)}, f32[3,8192]{1,0:T(4,128)}, s32[]{:T(128)}, /*index=5*/bf16[4,8192,128...) while((s32[]{:T(128)}, f32[512,128]{0,1:T(8,128)S(1)}, ...), condition=%wide.region_2.3_spmd.clone, body=%wide.region_0.2_spmd.clone.sunk | while | flops 483791392 | bytes 75739464 | solution.py:58
  15.8 3.3 pad_maximum_fusion.4
  19.8 5.2 fusion.23
  25.0 5.9 copy.25
  38.8 3.3 pad_maximum_fusion.4
  42.8 5.2 fusion.23
  47.9 5.9 copy.25
  61.8 3.3 pad_maximum_fusion.4
  65.7 5.2 fusion.23
  70.9 5.9 copy.25
  84.7 3.3 pad_maximum_fusion.4
  88.7 5.2 fusion.23
  93.9 5.9 copy.25
  107.7 3.3 pad_maximum_fusion.4
  111.7 5.2 fusion.23
  116.9 5.9 copy.25
  130.7 3.3 pad_maximum_fusion.4
  134.7 5.2 fusion.23
  139.8 5.9 copy.25
  153.7 3.3 pad_maximum_fusion.4
  157.6 5.2 fusion.23
  162.8 5.9 copy.25
  176.6 3.3 pad_maximum_fusion.4
  180.6 5.2 fusion.23
  185.8 5.9 copy.25
  199.6 3.3 pad_maximum_fusion.4
  203.6 5.2 fusion.23
  208.8 5.9 copy.25
  222.6 3.3 pad_maximum_fusion.4
  226.6 5.2 fusion.23
  231.7 5.9 copy.25
  245.6 3.3 pad_maximum_fusion.4
  249.5 5.2 fusion.23
  254.7 5.9 copy.25
  268.5 3.3 pad_maximum_fusion.4
  272.5 5.2 fusion.23
  277.7 5.9 copy.25
  295.5 5.2 fusion.23
  300.7 5.9 copy.25
  318.5 5.2 fusion.23
  323.6 5.9 copy.25
  341.4 5.2 fusion.23
  346.6 5.9 copy.25
  364.4 5.2 fusion.23
  369.6 5.9 copy.25
  383.4 328.7 %all-reduce.6.cloned.1.call-done = f32[512,128]{0,1:T(8,128)} async-done(((f32[512,128]{0,1:T(8,128)}), f32[512,128]{0,1:T(8,128)}) %all-reduce.6.cloned.1.call-update) | async-done | bytes 262160
  713.7 39.6 %reduce-scatter.4.cloned.1.call-done = f32[128,4]{1,0:T(8,128)} async-done(((f32[512,4]{1,0:T(8,128)}), f32[128,4]{1,0:T(8,128)}) %reduce-scatter.4.cloned.1.call-update) | async-done | bytes 2064
  (339 shorter events, 152.9 us)
Async XLA Ops:
  6.5 705.5 %all-reduce.6.cloned.1.call-start = ((), (), s32[]{:S(2)}) async-start(), calls=%async_computation.2 | async-start | bytes 524288
  13.8 368.4 %copy-start.2 = (u32[128]{0:T(128)S(1)}, u32[128]{0:T(128)}, u32[]{:S(2)}) copy-start(u32[128]{0:T(128)} %constant.132) | copy-start | bytes 1540
  31.9 2.2 copy-start
  54.9 2.2 copy-start
  77.9 2.2 copy-start
  100.8 2.2 copy-start
  123.8 2.2 copy-start
  146.8 2.2 copy-start
  169.8 2.2 copy-start
  192.7 2.2 copy-start
  215.7 2.2 copy-start
  238.7 2.2 copy-start
  261.7 2.2 copy-start
  284.6 2.2 copy-start
  307.6 2.2 copy-start
  330.6 2.2 copy-start
  353.6 2.2 copy-start
  376.5 2.2 copy-start
  381.4 0.7 copy-start.1
  382.1 371.1 %reduce-scatter.4.cloned.1.call-start = ((), (), s32[]{:S(2)}) async-start(), calls=%async_computation.1 | async-start | bytes 327680
Sparse Core Ops, SparseCore 0:
  382.2 329.7 all-reduce.5
  714.6 38.6 reduce-scatter.3
where the time goes:
time: 765 us; the launch traced here: 762 us
  waiting for transfers between devices  368 us (48%)
  other arithmetic  178 us (23%)
  local copies, waits for them, and re-layouts  174 us (23%)
  matrix products  17.7 us (2%)
  between operations  14.1 us (2%)
    unnamed x4, waiting for transfers between devices  368 us
    dot_general x16, local copies, waits for them, and re-layouts, sub_term(): lax.dot_general(coeffs, chans, (((0,), (0,)), ((), ())), preferred_elemen...  95 us
    convert_element_type x16, other arithmetic, make_coeffs(): return (coeffs * valid[None, :, None]).astype(jnp.bfloat16)  82.9 us
    concatenate x16, other arithmetic, make_coeffs(): jnp.concatenate([inv[None], unit * (inv * inv)[None], unit * inv[None]], 0)  52.9 us
    dynamic_slice x16, local copies, waits for them, and re-layouts, one_sub(): piece = lax.dynamic_slice_in_dim(sources, first, FSUB, 1)  21.9 us
    gather x16, local copies, waits for them, and re-layouts, move(): return lax.dynamic_slice_in_dim(block, samples - shift, samples, 1)  18.8 us
    dot_general x16, matrix products, sub_term(): lax.dot_general(coeffs, chans, (((0,), (0,)), ((), ())), preferred_elemen...  17.7 us
    slice x16, local copies, waits for them, and re-layouts, make_channels(): loads = source_piece[1:4].astype(jnp.float32)  16.3 us
  transfers between devices with their start and end apart: 2, of which 2 were waited for; matrix products, arithmetic and copies ran while one was open for 0% of the time, Pallas kernels for 0%

commit v1 on v0

v1 whole, which is shorter than its diff:
```python
import functools
import jax, jax.numpy as jnp
from jax import lax
from jax.experimental import pallas as pl
from jax.experimental.pallas import tpu as pltpu
from jax.sharding import PartitionSpec as P
FSUB=512
PADR=8
def kernel(live_ref, off_ref, obs_ref, pos_ref, src_ref, out_ref, c_ref, lt_ref, pb_ref, acc_ref, p2_ref, *, nsub, sps, mxu_r2=False):
    step = pl.program_id(0)
    T = src_ref.shape[2]; O = obs_ref.shape[1]; NT = O // 256
    @pl.when(step == 0)
    def _():
        acc_ref[...] = jnp.zeros_like(acc_ref)
    live = live_ref[0]
    def prep(u):
        s = step * sps + u
        left = live - s * FSUB
        keep = lax.broadcasted_iota(jnp.int32, (T, FSUB), 1) < left
        for c in range(4):
            lt = src_ref[c, u*FSUB:(u+1)*FSUB, :].T
            lt_ref[u, :, c*FSUB:(c+1)*FSUB] = jnp.where(keep, lt.astype(jnp.float32), 0.0).astype(jnp.bfloat16)
        for j in range(3):
            row = pos_ref[j:j+1, u*FSUB:(u+1)*FSUB]
            pb_ref[u, j] = jnp.broadcast_to(row, (128, FSUB)).T
    def coeffs(u, n):
        for h in range(2):
            o0 = n*256 + h*128
            ob = [jnp.broadcast_to(obs_ref[j:j+1, o0:o0+128], (16, 128)) for j in range(3)]
            for r in range(0, FSUB, 16):
                d = [ob[j] - pb_ref[u, j, r:r+16, :] for j in range(3)]
                r2 = d[0]*d[0] + d[1]*d[1] + d[2]*d[2]
                inv = lax.rsqrt(r2)
                i2 = inv*inv
                i3 = (i2*inv).astype(jnp.bfloat16)
                i2 = i2.astype(jnp.bfloat16)
                db = [x.astype(jnp.bfloat16) for x in d]
                ln = slice(h*128, h*128+128)
                def put(c, v):
                    c_ref[u, n, c*FSUB + r:c*FSUB + r + 16, ln] = v
                put(0, inv.astype(jnp.bfloat16))
                for j in range(3):
                    put(1+j, db[j]*i3)
                    put(4+j, db[j]*i2)
    def mm(u, n):
        s = step * sps + u
        p13 = jnp.dot(lt_ref[u], c_ref[u, n, :4*FSUB, :], preferred_element_type=jnp.float32)
        p2 = jnp.dot(lt_ref[u, :, FSUB:], c_ref[u, n, 4*FSUB:, :], preferred_element_type=jnp.float32)
        for h in range(2):
            q = n*2+h
            off = off_ref[s, q]
            sl = slice(h*128, h*128+128)
            a = p13[:, sl]; b = p2[:, sl]
            p2_ref[u, q, PADR:PADR+T, :] = b
            v = a + p2_ref[u, q, PADR+1:PADR+T+1, :] - p2_ref[u, q, PADR-1:PADR+T-1, :]
            acc_ref[q, pl.ds(off, T), :] += v
    @pl.when(step == 0)
    def _():
        p2_ref[...] = jnp.zeros_like(p2_ref)
    @pl.when(step * sps * FSUB < live)
    def _():
        prev = None
        for u in range(sps):
            prep(u)
            for n in range(NT):
                coeffs(u, n)
                if prev is not None: mm(*prev)
                prev = (u, n)
        mm(*prev)
    @pl.when(step == pl.num_programs(0) - 1)
    def _():
        pw = out_ref.shape[1]
        for q in range(2*NT):
            for w in range(pw):
                out_ref[pl.ds(q, T // pw, stride=2*NT), w, :] = acc_ref[q, pl.ds(w, T // pw, stride=pw), :]
def call(src, pos, live, off, obs, sps=1, pw=4):
    F = src.shape[1]; T = src.shape[2]; O = obs.shape[1]
    nsub = F // FSUB; NT = O//256
    return pl.pallas_call(
        functools.partial(kernel, nsub=nsub, sps=sps),
        out_shape=jax.ShapeDtypeStruct((T // pw * (O // 128), pw, 128), jnp.float32),
        grid=(nsub//sps,),
        in_specs=[pl.BlockSpec(memory_space=pltpu.SMEM), pl.BlockSpec(memory_space=pltpu.SMEM),
                  pl.BlockSpec((3, O), lambda i: (0, 0)),
                  pl.BlockSpec((3, sps*FSUB), lambda i: (0, i)),
                  pl.BlockSpec((4, sps*FSUB, T), lambda i: (0, i, 0))],
        out_specs=pl.BlockSpec((T // pw * (O // 128), pw, 128), lambda i: (0, 0, 0)),
        scratch_shapes=[pltpu.VMEM((sps, NT, 7*FSUB, 256), jnp.bfloat16),
                        pltpu.VMEM((sps, T, 4*FSUB), jnp.bfloat16),
                        pltpu.VMEM((sps, 3, FSUB, 128), jnp.float32),
                        pltpu.VMEM((2*NT, T + 64, 128), jnp.float32),
                        pltpu.VMEM((sps, 2*NT, T + 2*PADR, 128), jnp.float32)],
        compiler_params=pltpu.CompilerParams(vmem_limit_bytes=56*1024*1024, dimension_semantics=("arbitrary",)),
    )(live, off, obs, pos, src)


def body(sources, positions, counts, offsets, observers):
    everyone = lax.all_gather(observers, "blk", axis=1, tiled=True)
    ngroup = lax.axis_size("group")
    pieces = call(sources, positions, counts, offsets, everyone, sps=2, pw=sources.shape[2] // ngroup)
    arrived = lax.all_to_all(pieces, ("group", "blk"), 0, 0, tiled=True)
    return (arrived.sum(0) * (1.0 / (4.0 * jnp.pi))).T


def solution(mesh):
    return jax.shard_map(
        body,
        mesh=mesh,
        in_specs=(
            P(None, ("group", "blk"), None),
            P(None, ("group", "blk")),
            P(("group", "blk")),
            P(("group", "blk"), None),
            P(None, "blk"),
        ),
        out_specs=P("blk", "group"),
        check_vma=False,
    )
```

time: 765 us -> 53.2 us (0.07)
  waiting for transfers between devices: 368 us -> 0 us
  other arithmetic: 178 us -> 0.73 us
  local copies, waits for them, and re-layouts: 174 us -> 1.35 us
  blocking collectives: 6.5 us -> 34.4 us
  matrix products: 17.7 us -> 0 us
  Pallas kernels: 0 us -> 16.1 us
  between operations: 14.1 us -> 0.66 us
    unnamed x4 -> x0, waiting for transfers between devices: 368 us -> none
    convert_element_type x48 -> x0, other arithmetic: 97.5 us -> none  [the longest x16 82.9 us: make_coeffs(): return (coeffs * valid[None, :, None]).astype(jnp.bfloat16)]
    dot_general x16 -> x0, local copies, waits for them, and re-layouts: 95 us -> none  [sub_term(): lax.dot_general(coeffs, chans, (((0,), (0,)), ((), ())), preferred_elemen...]
    concatenate x32 -> x0, other arithmetic: 54.2 us -> none  [the longest x16 52.9 us: make_coeffs(): jnp.concatenate([inv[None], unit * (inv * inv)[None], unit * inv[None]], 0)]
    dynamic_slice x32 -> x0, local copies, waits for them, and re-layouts: 33.2 us -> none  [the longest x16 21.9 us: one_sub(): piece = lax.dynamic_slice_in_dim(sources, first, FSUB, 1)]
    all_to_all x0 -> x1, blocking collectives: none -> 26.6 us  [body(): arrived = lax.all_to_all(pieces, ('group', 'blk'), 0, 0, tiled=True)]
    gather x16 -> x0, local copies, waits for them, and re-layouts: 18.8 us -> none  [move(): return lax.dynamic_slice_in_dim(block, samples - shift, samples, 1)]
    dot_general x16 -> x0, matrix products: 17.7 us -> none  [sub_term(): lax.dot_general(coeffs, chans, (((0,), (0,)), ((), ())), preferred_elemen...]
  transfers between devices with their start and end apart: 2 -> 0, of which waited for: 2 -> 0; matrix products, arithmetic and copies ran while one was open for 0% -> 0% of each run, Pallas kernels for 0% -> 0%
where the time goes in v1:
time: 53.2 us; the launch traced here: 53.3 us
  blocking collectives  34.4 us (65%)
  Pallas kernels  16.1 us (30%)
  local copies, waits for them, and re-layouts  1.35 us (3%)
  other arithmetic  0.73 us (1%)
  between operations  0.66 us (1%)
    all_to_all x1, blocking collectives, body(): arrived = lax.all_to_all(pieces, ('group', 'blk'), 0, 0, tiled=True)  26.6 us
    pallas_call x1, Pallas kernels, call(): pl.pallas_call(functools.partial(kernel, nsub=nsub, sps=sps), out_shape=j...  16.1 us
    all_gather x1, blocking collectives, body(): everyone = lax.all_gather(observers, 'blk', axis=1, tiled=True)  7.79 us
    unnamed x1, local copies, waits for them, and re-layouts  1.35 us

profile of v1, /device:TPU:1, one launch (start us, length us, event | category | flops | bytes accessed | tf_op | source)
XLA Modules:
  0.0 53.3 jit_solution(12175902359755867759)
XLA Ops:
  0.7 1.3 %copy.6.off_ref = s32[16,4]{1,0:T(8,128)} copy(s32[16,4]{0,1:T(4,128)} %param.8) | data formatting | bytes 512 | tf_op args[3]
  2.0 7.8 %all_gather.3.obs_ref = f32[3,512]{1,0:T(4,128)} all-gather(f32[3,128]{1,0:T(4,128)} %param.9), channel_id=1, replica_groups=mesh['group'=32,'blk'=4] {'blk'}, dimensions={1}, use_global_device_ids=true | all-gather | bytes 7680 | tf_op jit(solution)/shard_map/all_gather | solution.py:98
  9.8 16.1 %shard_map.55 = f32[128,4,128]{2,1,0:T(4,128)} custom-call(s32[1]{0:T(128)S(6)} %copy.7.live_ref, s32[16,4]{1,0:T(8,128)} %copy.6.off_ref, f32[3,512]{1,0:T(4,128)} %all_gather.3.obs_ref, f32[3,8192]{1,0:T(4,128)} %pos_ref.1, bf16[4,8192,128]{2,1,0:T(8,128)(2,1)} %src_ref.1), custom_call_target="tpu_custom_call" | custom-call | tf_op jit(solution)/shard_map/pallas_call | solution.py:79
  25.9 26.6 %all_to_all.5 = f32[128,4,128]{2,1,0:T(4,128)S(1)} all-to-all(f32[128,4,128]{2,1,0:T(4,128)} %shard_map.55), channel_id=1, replica_groups=mesh['group'=32,'blk'=4] {'group','blk'}, dimensions={0} | all-to-all | bytes 524288 | tf_op jit(solution)/shard_map/all_to_all | solution.py:101
  52.6 0.1 reduce_sum.9
  52.7 0.6 %multiply_bitcast_fusion = f32[128,4]{0,1:T(4,128)} fusion(f32[4,128]{1,0:T(4,128)S(1)} %reduce_sum.9), kind=kLoop, calls=%fused_computation | loop fusion | flops 512 | bytes 4096 | tf_op jit(solution)/shard_map/mul | solution.py:102

commit v2 on v0

v2 whole, which is shorter than its diff:
```python
import functools
import jax, jax.numpy as jnp
from jax import lax
from jax.experimental import pallas as pl
from jax.experimental.pallas import tpu as pltpu
from jax.sharding import PartitionSpec as P
FSUB=512
PADR=8
CH=64
U=2
AHEAD=4
def signal_kernel(live_hbm, off_hbm, *rest, nob, T, nsub, pw):
    obs_any = rest[:nob]
    pos_hbm, src_hbm, out_ref = rest[nob:nob+3]
    live_s, off_s, obs_v, pos_v, src_v, lt_ref, pb_ref, acc_ref, p2_ref, sem, ssem = rest[nob+3:]
    NT = nob // 2
    me = lax.axis_index("blk")
    NP = FSUB // (2*CH)
    small = [pltpu.make_async_copy(live_hbm, live_s, sem.at[0]),
             pltpu.make_async_copy(off_hbm, off_s, sem.at[1]),
             pltpu.make_async_copy(pos_hbm, pos_v, sem.at[2])]
    views = [pltpu.make_async_copy(obs_any[m], obs_v.at[m], sem.at[3+m]) for m in range(nob)]
    def load(s):
        return pltpu.make_async_copy(src_hbm.at[:, pl.ds(pl.multiple_of(s*FSUB, FSUB), FSUB), :], src_v.at[s], ssem.at[s])
    small[0].start()
    small[2].start()
    load(0).start()
    small[1].start()
    for c in views: c.start()
    load(1).start()
    acc_ref[...] = jnp.zeros_like(acc_ref)
    for m in range(nob):
        for u in range(U):
            p2_ref[u, m, 0:PADR, :] = jnp.zeros((PADR, 128), jnp.float32)
            p2_ref[u, m, PADR+T:, :] = jnp.zeros((PADR, 128), jnp.float32)
    small[0].wait()
    live = live_s[0]
    nlive = lax.div(live + FSUB - 1, FSUB)
    for s in range(2, AHEAD):
        @pl.when(s < nlive)
        def _(): load(s).start()
    def prep(s, kk):
        for e in range(2):
            f0 = (2*kk+e)*CH
            x = jnp.concatenate([src_v[s, c, f0:f0+CH, :] for c in (1, 2, 3, 0)], 0)
            lt_ref[2*kk+e] = x.T
        for j in range(3):
            row = pos_v[j:j+1, pl.ds(pl.multiple_of(s*FSUB+kk*2*CH, 2*CH), 2*CH)]
            pb_ref[kk, j] = jnp.broadcast_to(row, (128, 2*CH)).T
    def coeffs(k, n):
        cols = [[[], []] for _ in range(7)]
        for h in range(2):
            ob = [jnp.broadcast_to(obs_v[2*n+h, j:j+1, :], (16, 128)) for j in range(3)]
            for r in range(0, CH, 16):
                r0 = (k % 2)*CH + r
                d = [ob[j] - pb_ref[k//2, j, r0:r0+16, :] for j in range(3)]
                r2 = d[0]*d[0] + d[1]*d[1] + d[2]*d[2]
                inv = lax.rsqrt(r2)
                i2 = inv*inv
                i3 = (i2*inv).astype(jnp.bfloat16)
                i2 = i2.astype(jnp.bfloat16)
                db = [x.astype(jnp.bfloat16) for x in d]
                for j in range(3):
                    cols[j][h].append(db[j]*i3)
                    cols[4+j][h].append(db[j]*i2)
                cols[3][h].append(inv.astype(jnp.bfloat16))
        def whole(cs, pad):
            halves = []
            for h in range(2):
                rows = [v for c in cs for v in cols[c][h]]
                if pad: rows.append(jnp.zeros((pad, 128), jnp.bfloat16))
                halves.append(jnp.concatenate(rows, 0))
            return jnp.concatenate(halves, 1)
        return whole(range(4), 0), whole(range(4, 7), CH)
    def finish(s, u, n, p13, p2):
        for h in range(2):
            m = n*2+h
            off = off_s[me ^ m, s]
            sl = slice(h*128, h*128+128)
            p2_ref[u, m, PADR:PADR+T, :] = p2[:, sl]
            v = p13[:, sl] + p2_ref[u, m, PADR+1:PADR+T+1, :] - p2_ref[u, m, PADR-1:PADR+T-1, :]
            acc_ref[m, pl.ds(off, T), :] += v
    def cut(s):
        left = live - s*FSUB
        @pl.when(left < FSUB)
        def _():
            face = lax.broadcasted_iota(jnp.int32, (FSUB, T), 0)
            for c in range(4):
                v = src_v[s, c].astype(jnp.float32)
                src_v[s, c] = jnp.where(face < left, v, 0.0).astype(jnp.bfloat16)
    small[2].wait()
    load(0).wait()
    prep(0, 0)
    small[1].wait()
    for c in views: c.wait()
    ngrp = lax.div(nlive + U - 1, U)
    def body(i, _):
        for u in range(U):
            s = U*i + u
            nxt = jnp.minimum(s + 1, nsub - 1)
            @pl.when((s + 1 < nlive))
            def _(): load(s+1).wait()
            @pl.when((s + AHEAD < nlive))
            def _(): load(s+AHEAD).start()
            @pl.when(s + 1 < nsub)
            def _(): cut(s + 1)
        for u in range(U):
            s = U*i + u
            nxt = jnp.minimum(s + 1, nsub - 1)
            p = [[None, None] for _ in range(NT)]
            for kk in range(NP):
                if kk + 1 < NP: prep(s, kk + 1)
                else: prep(nxt, 0)
                for k in (2*kk, 2*kk+1):
                    lt = lt_ref[k]
                    for n in range(NT):
                        cs = coeffs(k, n)
                        for e in range(2):
                            y = jnp.dot(lt, cs[e], preferred_element_type=jnp.float32)
                            p[n][e] = y if k == 0 else p[n][e] + y
            for n in range(NT): finish(s, u, n, *p[n])
        return 0
    lax.fori_loop(0, ngrp, body, 0)
    for m in range(nob):
        for w in range(pw):
            out_ref[pl.ds(me ^ m, T // pw, stride=nob), w, :] = acc_ref[m, pl.ds(w, T // pw, stride=pw), :] * (1.0 / (4.0 * jnp.pi))
def face_signals(src, pos, live, off, obs, pw):
    F = src.shape[1]; T = src.shape[2]
    nob = len(obs); nsub = F // FSUB
    A = pl.BlockSpec(memory_space=pl.ANY)
    H = pl.BlockSpec(memory_space=pltpu.HBM)
    V = pl.BlockSpec(memory_space=pltpu.VMEM)
    return pl.pallas_call(
        functools.partial(signal_kernel, nob=nob, T=T, nsub=nsub, pw=pw),
        out_shape=jax.ShapeDtypeStruct((T // pw * nob, pw, 128), jnp.float32),
        in_specs=[H, H] + [A]*nob + [H, H],
        out_specs=V,
        scratch_shapes=[pltpu.SMEM(live.shape, jnp.int32), pltpu.SMEM(off.shape, jnp.int32),
                        pltpu.VMEM((nob,) + obs[0].shape, jnp.float32),
                        pltpu.VMEM(pos.shape, jnp.float32),
                        pltpu.VMEM((nsub, 4, FSUB, T), jnp.bfloat16),
                        pltpu.VMEM((FSUB//CH, T, 4*CH), jnp.bfloat16),
                        pltpu.VMEM((FSUB//CH//2, 3, 2*CH, 128), jnp.float32),
                        pltpu.VMEM((nob, T + 64, 128), jnp.float32),
                        pltpu.VMEM((U, nob, T + 2*PADR, 128), jnp.float32),
                        pltpu.SemaphoreType.DMA((3 + nob,)), pltpu.SemaphoreType.DMA((nsub,))],
        compiler_params=pltpu.CompilerParams(vmem_limit_bytes=24*1024*1024),
    )(live, off, *obs, pos, src)


def body(sources, positions, counts, offsets, observers):
    nblk = lax.axis_size("blk")
    others = [lax.ppermute(observers, "blk", [(i, i ^ m) for i in range(nblk)]) for m in range(1, nblk)]
    pieces = face_signals(sources, positions, counts, offsets.T, [observers] + others, sources.shape[2] // lax.axis_size("group"))
    arrived = lax.all_to_all(pieces, ("group", "blk"), 0, 0, tiled=True)
    return arrived.sum(0).T


def solution(mesh):
    return jax.shard_map(
        body,
        mesh=mesh,
        in_specs=(
            P(None, ("group", "blk"), None),
            P(None, ("group", "blk")),
            P(("group", "blk")),
            P(("group", "blk"), None),
            P(None, "blk"),
        ),
        out_specs=P("blk", "group"),
        check_vma=False,
    )
```

time: 765 us -> 43.3 us (0.06)
  waiting for transfers between devices: 368 us -> 2.5 us
  other arithmetic: 178 us -> 0.72 us
  local copies, waits for them, and re-layouts: 174 us -> 5.65 us
  matrix products: 17.7 us -> 0 us
  blocking collectives: 6.5 us -> 21.6 us
  between operations: 14.1 us -> 0.68 us
  Pallas kernels: 0 us -> 9.35 us
    unnamed x4 -> x0, waiting for transfers between devices: 368 us -> none
    convert_element_type x48 -> x0, other arithmetic: 97.5 us -> none  [the longest x16 82.9 us: make_coeffs(): return (coeffs * valid[None, :, None]).astype(jnp.bfloat16)]
    dot_general x16 -> x0, local copies, waits for them, and re-layouts: 95 us -> none  [sub_term(): lax.dot_general(coeffs, chans, (((0,), (0,)), ((), ())), preferred_elemen...]
    concatenate x32 -> x0, other arithmetic: 54.2 us -> none  [the longest x16 52.9 us: make_coeffs(): jnp.concatenate([inv[None], unit * (inv * inv)[None], unit * inv[None]], 0)]
    dynamic_slice x32 -> x0, local copies, waits for them, and re-layouts: 33.2 us -> none  [the longest x16 21.9 us: one_sub(): piece = lax.dynamic_slice_in_dim(sources, first, FSUB, 1)]
    all_to_all x0 -> x1, blocking collectives: none -> 21.6 us  [body(): arrived = lax.all_to_all(pieces, ('group', 'blk'), 0, 0, tiled=True)]
    gather x16 -> x0, local copies, waits for them, and re-layouts: 18.8 us -> none  [move(): return lax.dynamic_slice_in_dim(block, samples - shift, samples, 1)]
    dot_general x16 -> x0, matrix products: 17.7 us -> none  [sub_term(): lax.dot_general(coeffs, chans, (((0,), (0,)), ((), ())), preferred_elemen...]
  transfers between devices with their start and end apart: 2 -> 3, of which waited for: 2 -> 2; matrix products, arithmetic and copies ran while one was open for 0% -> 0% of each run, Pallas kernels for 0% -> 0%
where the time goes in v2:
time: 43.3 us; the launch traced here: 43.6 us
  blocking collectives  21.6 us (50%)
  Pallas kernels  9.35 us (22%)
  local copies, waits for them, and re-layouts  5.65 us (13%)
  starting transfers between devices  3.06 us (7%)
  waiting for transfers between devices  2.5 us (6%)
  other arithmetic  0.72 us (2%)
  between operations  0.68 us (2%)
    all_to_all x1, blocking collectives, body(): arrived = lax.all_to_all(pieces, ('group', 'blk'), 0, 0, tiled=True)  21.6 us
    pallas_call x1, Pallas kernels, face_signals(): pl.pallas_call(functools.partial(signal_kernel, nob=nob, T=T, nsub=nsub,...  9.35 us
    unnamed x8, local copies, waits for them, and re-layouts  5.65 us
    ppermute x3, starting transfers between devices, body(): lax.ppermute(observers, 'blk', [(i, i ^ m) for i in range(nblk)])  3.06 us
    ppermute x3, waiting for transfers between devices, body(): lax.ppermute(observers, 'blk', [(i, i ^ m) for i in range(nblk)])  2.5 us
  transfers between devices with their start and end apart: 3, of which 2 were waited for; matrix products, arithmetic and copies ran while one was open for 0% of the time, Pallas kernels for 0%

profile of v2, /device:TPU:1, one launch (start us, length us, event | category | flops | bytes accessed | tf_op | source)
XLA Modules:
  0.0 43.6 jit_solution(15456081875177686096)
XLA Ops:
  0.0 2.0 %collective-permute-start.1 = (f32[3,128]{1,0:T(4,128)}, f32[3,128]{1,0:T(4,128)S(1)}, u32[]{:S(2)}, u32[]{:S(2)}) collective-permute-start(f32[3,128]{1,0:T(4,128)} %rest_0_.1), channel_id=1, source_target_pairs={{0,2},{1,3},{2,0},{3,1},{4,6},{5,7},{6,4},{7,5},{8,10},{9,11},{10,... | collective-permute-start | bytes 4616 | tf_op jit(solution)/shard_map/ppermute | solution.py:153
  2.0 1.0 %collective-permute-start = (f32[3,128]{1,0:T(4,128)}, f32[3,128]{1,0:T(4,128)S(1)}, u32[]{:S(2)}, u32[]{:S(2)}) collective-permute-start(f32[3,128]{1,0:T(4,128)} %rest_0_.1), channel_id=1, source_target_pairs={{0,1},{1,0},{2,3},{3,2},{4,5},{5,4},{6,7},{7,6},{8,9},{9,8},{10,11... | collective-permute-start | bytes 4616 | tf_op jit(solution)/shard_map/ppermute | solution.py:153
  3.0 0.1 collective-permute-start.2
  3.7 0.0 collective-permute-done.1.rest_2_
  3.7 0.3 collective-permute-done.rest_1_
  4.0 2.2 %collective-permute-done.2.rest_3_ = f32[3,128]{1,0:T(4,128)S(1)} collective-permute-done((f32[3,128]{1,0:T(4,128)}, f32[3,128]{1,0:T(4,128)S(1)}, u32[]{:S(2)}, u32[]{:S(2)}) %collective-permute-start.2) | collective-permute-done | bytes 1568 | tf_op jit(solution)/shard_map/ppermute | solution.py:153
  6.2 0.0 copy-start
  6.2 3.4 %copy-done = bf16[4,8192,128]{2,1,0:T(8,128)(2,1)S(1)} copy-done((bf16[4,8192,128]{2,1,0:T(8,128)(2,1)S(1)}, bf16[4,8192,128]{2,1,0:T(8,128)(2,1)}, u32[]{:S(2)}) %copy-start) | copy-done | bytes 8388632
  9.6 0.0 copy-start.1
  9.6 0.9 %copy-done.1 = f32[3,8192]{1,0:T(4,128)S(1)} copy-done((f32[3,8192]{1,0:T(4,128)S(1)}, f32[3,8192]{1,0:T(4,128)}, u32[]{:S(2)}) %copy-start.1) | copy-done | bytes 98328
  10.5 0.0 copy-start.2
  10.5 0.7 %copy-done.2 = s32[16,4]{0,1:T(4,128)S(1)} copy-done((s32[16,4]{0,1:T(4,128)S(1)}, s32[16,4]{0,1:T(4,128)}, u32[]{:S(2)}) %copy-start.2) | copy-done | bytes 280
  11.2 0.0 copy-start.3
  11.2 0.7 %copy-done.3 = f32[3,128]{1,0:T(4,128)S(1)} copy-done((f32[3,128]{1,0:T(4,128)S(1)}, f32[3,128]{1,0:T(4,128)}, u32[]{:S(2)}) %copy-start.3) | copy-done | bytes 1560
  11.9 9.3 %shard_map.55 = f32[128,4,128]{2,1,0:T(4,128)S(1)} custom-call(s32[1]{0:T(128)S(6)} %copy.6.live_hbm, s32[4,16]{1,0:T(4,128)S(1)} %bitcast.2, f32[3,128]{1,0:T(4,128)S(1)} %copy-done.3, f32[3,128]{1,0:T(4,128)S(1)} %collective-permute-done.rest_1_, f32[3,128]{1,0:T(4,128)S(1)} %collective-permute-done.1.rest_2_, ...), custom_call_target="tpu_custom_call" | custom-call | tf_op jit(solution)/shard_map/pallas_call | solution.py:133
  21.2 21.6 %all_to_all.5 = f32[128,4,128]{2,1,0:T(4,128)S(1)} all-to-all(f32[128,4,128]{2,1,0:T(4,128)S(1)} %shard_map.55), channel_id=1, replica_groups=mesh['group'=32,'blk'=4] {'group','blk'}, dimensions={0} | all-to-all | bytes 524288 | tf_op jit(solution)/shard_map/all_to_all | solution.py:155
  42.9 0.7 %reduce_sum.9 = f32[4,128]{1,0:T(4,128)} reduce(f32[128,4,128]{2,1,0:T(4,128)S(1)} %all_to_all.5, f32[]{:T(128)} %constant.0.clone.1), dimensions={0}, to_apply=%region_0.0 | reduce | flops 65024 | bytes 264196 | tf_op jit(solution)/shard_map/reduce_sum | solution.py:156
Async XLA Ops:
  0.0 3.7 %collective-permute-start.1 = (f32[3,128]{1,0:T(4,128)}, f32[3,128]{1,0:T(4,128)S(1)}, u32[]{:S(2)}, u32[]{:S(2)}) collective-permute-start(f32[3,128]{1,0:T(4,128)} %rest_0_.1), channel_id=1, source_target_pairs={{0,2},{1,3},{2,0},{3,1},{4,6},{5,7},{6,4},{7,5},{8,10},{9,11},{10,... | collective-permute-start | bytes 4616 | tf_op jit(solution)/shard_map/ppermute | solution.py:153
  2.0 2.0 %collective-permute-start = (f32[3,128]{1,0:T(4,128)}, f32[3,128]{1,0:T(4,128)S(1)}, u32[]{:S(2)}, u32[]{:S(2)}) collective-permute-start(f32[3,128]{1,0:T(4,128)} %rest_0_.1), channel_id=1, source_target_pairs={{0,1},{1,0},{2,3},{3,2},{4,5},{5,4},{6,7},{7,6},{8,9},{9,8},{10,11... | collective-permute-start | bytes 4616 | tf_op jit(solution)/shard_map/ppermute | solution.py:153
  3.0 3.2 %collective-permute-start.2 = (f32[3,128]{1,0:T(4,128)}, f32[3,128]{1,0:T(4,128)S(1)}, u32[]{:S(2)}, u32[]{:S(2)}) collective-permute-start(f32[3,128]{1,0:T(4,128)} %rest_0_.1), channel_id=1, source_target_pairs={{0,3},{1,2},{2,1},{3,0},{4,7},{5,6},{6,5},{7,4},{8,11},{9,10},{10,... | collective-permute-start | bytes 4616 | tf_op jit(solution)/shard_map/ppermute | solution.py:153
  6.2 3.4 %copy-start = (bf16[4,8192,128]{2,1,0:T(8,128)(2,1)S(1)}, bf16[4,8192,128]{2,1,0:T(8,128)(2,1)}, u32[]{:S(2)}) copy-start(bf16[4,8192,128]{2,1,0:T(8,128)(2,1)} %rest_5_.1) | copy-start | bytes 25165828
  9.6 0.9 %copy-start.1 = (f32[3,8192]{1,0:T(4,128)S(1)}, f32[3,8192]{1,0:T(4,128)}, u32[]{:S(2)}) copy-start(f32[3,8192]{1,0:T(4,128)} %rest_4_.1) | copy-start | bytes 294916
  10.5 0.7 %copy-start.2 = (s32[16,4]{0,1:T(4,128)S(1)}, s32[16,4]{0,1:T(4,128)}, u32[]{:S(2)}) copy-start(s32[16,4]{0,1:T(4,128)} %param.8) | copy-start | bytes 772
  11.2 0.7 %copy-start.3 = (f32[3,128]{1,0:T(4,128)S(1)}, f32[3,128]{1,0:T(4,128)}, u32[]{:S(2)}) copy-start(f32[3,128]{1,0:T(4,128)} %rest_0_.1) | copy-start | bytes 4612

commit v3 on v2

--- a/solution.py
+++ b/solution.py
@@ -56,14 +56,14 @@
                 d = [ob[j] - pb_ref[k//2, j, r0:r0+16, :] for j in range(3)]
                 r2 = d[0]*d[0] + d[1]*d[1] + d[2]*d[2]
                 inv = lax.rsqrt(r2)
-                i2 = inv*inv
-                i3 = (i2*inv).astype(jnp.bfloat16)
-                i2 = i2.astype(jnp.bfloat16)
+                i2 = pl.reciprocal(r2, approx=True).astype(jnp.bfloat16)
+                ib = inv.astype(jnp.bfloat16)
                 db = [x.astype(jnp.bfloat16) for x in d]
                 for j in range(3):
-                    cols[j][h].append(db[j]*i3)
-                    cols[4+j][h].append(db[j]*i2)
-                cols[3][h].append(inv.astype(jnp.bfloat16))
+                    t2 = db[j]*i2
+                    cols[j][h].append(t2*ib)
+                    cols[4+j][h].append(t2)
+                cols[3][h].append(ib)
         def whole(cs, pad):
             halves = []
             for h in range(2):
@@ -115,7 +115,7 @@
                     lt = lt_ref[k]
                     for n in range(NT):
                         cs = coeffs(k, n)
-                        for e in range(2):
+                        for e in (1, 0):
                             y = jnp.dot(lt, cs[e], preferred_element_type=jnp.float32)
                             p[n][e] = y if k == 0 else p[n][e] + y
             for n in range(NT): finish(s, u, n, *p[n])
@@ -144,7 +144,7 @@
                         pltpu.VMEM((nob, T + 64, 128), jnp.float32),
                         pltpu.VMEM((U, nob, T + 2*PADR, 128), jnp.float32),
                         pltpu.SemaphoreType.DMA((3 + nob,)), pltpu.SemaphoreType.DMA((nsub,))],
-        compiler_params=pltpu.CompilerParams(vmem_limit_bytes=24*1024*1024),
+        compiler_params=pltpu.CompilerParams(vmem_limit_bytes=54*1024*1024),
     )(live, off, *obs, pos, src)
 
 

time: 43.3 us -> 39.5 us (0.912)
  local copies, waits for them, and re-layouts: 5.65 us -> 0.59 us
  blocking collectives: 21.6 us -> 22.6 us
    unnamed x8 -> x6, local copies, waits for them, and re-layouts: 5.65 us -> 0.59 us
    all_to_all x1, blocking collectives: 21.6 us -> 22.6 us  [body(): arrived = lax.all_to_all(pieces, ('group', 'blk'), 0, 0, tiled=True)]
where the time goes in v3:
time: 39.5 us; the launch traced here: 39.8 us
  blocking collectives  22.6 us (57%)
  Pallas kernels  9.67 us (24%)
  starting transfers between devices  3.06 us (8%)
  waiting for transfers between devices  2.49 us (6%)
  other arithmetic  0.72 us (2%)
  between operations  0.68 us (2%)
  local copies, waits for them, and re-layouts  0.59 us (1%)
    all_to_all x1, blocking collectives, body(): arrived = lax.all_to_all(pieces, ('group', 'blk'), 0, 0, tiled=True)  22.6 us
    pallas_call x1, Pallas kernels, face_signals(): pl.pallas_call(functools.partial(signal_kernel, nob=nob, T=T, nsub=nsub,...  9.67 us
    ppermute x3, starting transfers between devices, body(): lax.ppermute(observers, 'blk', [(i, i ^ m) for i in range(nblk)])  3.06 us
    ppermute x3, waiting for transfers between devices, body(): lax.ppermute(observers, 'blk', [(i, i ^ m) for i in range(nblk)])  2.49 us
  transfers between devices with their start and end apart: 3, of which 2 were waited for; matrix products, arithmetic and copies ran while one was open for 0% of the time, Pallas kernels for 0%

profile of v3, /device:TPU:1, one launch (start us, length us, event | category | flops | bytes accessed | tf_op | source)
XLA Modules:
  0.0 39.8 jit_solution(12421898210924065517)
XLA Ops:
  0.0 2.0 %collective-permute-start.1 = (f32[3,128]{1,0:T(4,128)}, f32[3,128]{1,0:T(4,128)S(1)}, u32[]{:S(2)}, u32[]{:S(2)}) collective-permute-start(f32[3,128]{1,0:T(4,128)} %rest_0_.1), channel_id=1, source_target_pairs={{0,2},{1,3},{2,0},{3,1},{4,6},{5,7},{6,4},{7,5},{8,10},{9,11},{10,... | collective-permute-start | bytes 4616 | tf_op jit(solution)/shard_map/ppermute | solution.py:153
  2.0 1.0 %collective-permute-start = (f32[3,128]{1,0:T(4,128)}, f32[3,128]{1,0:T(4,128)S(1)}, u32[]{:S(2)}, u32[]{:S(2)}) collective-permute-start(f32[3,128]{1,0:T(4,128)} %rest_0_.1), channel_id=1, source_target_pairs={{0,1},{1,0},{2,3},{3,2},{4,5},{5,4},{6,7},{7,6},{8,9},{9,8},{10,11... | collective-permute-start | bytes 4616 | tf_op jit(solution)/shard_map/ppermute | solution.py:153
  3.0 0.1 collective-permute-start.2
  3.7 0.0 collective-permute-done.1.rest_2_
  3.7 0.0 copy-start
  3.7 0.3 collective-permute-done.rest_1_
  4.0 0.0 copy-start.1
  4.0 2.2 %collective-permute-done.2.rest_3_ = f32[3,128]{1,0:T(4,128)S(1)} collective-permute-done((f32[3,128]{1,0:T(4,128)}, f32[3,128]{1,0:T(4,128)S(1)}, u32[]{:S(2)}, u32[]{:S(2)}) %collective-permute-start.2) | collective-permute-done | bytes 1568 | tf_op jit(solution)/shard_map/ppermute | solution.py:153
  6.2 0.0 copy-start.2
  6.2 0.0 copy-done
  6.2 0.0 copy-done.1
  6.2 0.6 %copy-done.2 = f32[3,128]{1,0:T(4,128)} copy-done((f32[3,128]{1,0:T(4,128)}, f32[3,128]{1,0:T(4,128)S(1)}, u32[]{:S(2)}) %copy-start.2) | copy-done | bytes 1560
  6.8 9.7 %shard_map.55 = f32[128,4,128]{2,1,0:T(4,128)} custom-call(s32[1]{0:T(128)S(6)} %copy.6.live_hbm, s32[4,16]{1,0:T(4,128)} %bitcast.2, f32[3,128]{1,0:T(4,128)} %rest_0_.1, f32[3,128]{1,0:T(4,128)} %copy-done.1, f32[3,128]{1,0:T(4,128)} %copy-done, f32[3,128]{1,0:T(4,128)} %copy-done.2, f32[3,8192]{1,0:T(4,128)} %rest_4_.1, bf16[4,8192,128]{2,1,0:T(8,128)(2,1)} %rest_5_.1), custom_call_target="tpu_custom_call" | custom-call | tf_op jit(solution)/shard_map/pallas_call | solution.py:133
  16.5 22.6 %all_to_all.5 = f32[128,4,128]{2,1,0:T(4,128)S(1)} all-to-all(f32[128,4,128]{2,1,0:T(4,128)} %shard_map.55), channel_id=1, replica_groups=mesh['group'=32,'blk'=4] {'group','blk'}, dimensions={0} | all-to-all | bytes 524288 | tf_op jit(solution)/shard_map/all_to_all | solution.py:155
  39.1 0.7 %reduce_sum.9 = f32[4,128]{1,0:T(4,128)} reduce(f32[128,4,128]{2,1,0:T(4,128)S(1)} %all_to_all.5, f32[]{:T(128)} %constant.0.clone.1), dimensions={0}, to_apply=%region_0.0 | reduce | flops 65024 | bytes 264196 | tf_op jit(solution)/shard_map/reduce_sum | solution.py:156
Async XLA Ops:
  0.0 3.7 %collective-permute-start.1 = (f32[3,128]{1,0:T(4,128)}, f32[3,128]{1,0:T(4,128)S(1)}, u32[]{:S(2)}, u32[]{:S(2)}) collective-permute-start(f32[3,128]{1,0:T(4,128)} %rest_0_.1), channel_id=1, source_target_pairs={{0,2},{1,3},{2,0},{3,1},{4,6},{5,7},{6,4},{7,5},{8,10},{9,11},{10,... | collective-permute-start | bytes 4616 | tf_op jit(solution)/shard_map/ppermute | solution.py:153
  2.0 2.0 %collective-permute-start = (f32[3,128]{1,0:T(4,128)}, f32[3,128]{1,0:T(4,128)S(1)}, u32[]{:S(2)}, u32[]{:S(2)}) collective-permute-start(f32[3,128]{1,0:T(4,128)} %rest_0_.1), channel_id=1, source_target_pairs={{0,1},{1,0},{2,3},{3,2},{4,5},{5,4},{6,7},{7,6},{8,9},{9,8},{10,11... | collective-permute-start | bytes 4616 | tf_op jit(solution)/shard_map/ppermute | solution.py:153
  3.0 3.2 %collective-permute-start.2 = (f32[3,128]{1,0:T(4,128)}, f32[3,128]{1,0:T(4,128)S(1)}, u32[]{:S(2)}, u32[]{:S(2)}) collective-permute-start(f32[3,128]{1,0:T(4,128)} %rest_0_.1), channel_id=1, source_target_pairs={{0,3},{1,2},{2,1},{3,0},{4,7},{5,6},{6,5},{7,4},{8,11},{9,10},{10,... | collective-permute-start | bytes 4616 | tf_op jit(solution)/shard_map/ppermute | solution.py:153
  3.7 2.5 %copy-start = (f32[3,128]{1,0:T(4,128)}, f32[3,128]{1,0:T(4,128)S(1)}, u32[]{:S(2)}) copy-start(f32[3,128]{1,0:T(4,128)S(1)} %collective-permute-done.1.rest_2_) | copy-start | bytes 4612
  4.0 2.2 %copy-start.1 = (f32[3,128]{1,0:T(4,128)}, f32[3,128]{1,0:T(4,128)S(1)}, u32[]{:S(2)}) copy-start(f32[3,128]{1,0:T(4,128)S(1)} %collective-permute-done.rest_1_) | copy-start | bytes 4612
  6.2 0.6 %copy-start.2 = (f32[3,128]{1,0:T(4,128)}, f32[3,128]{1,0:T(4,128)S(1)}, u32[]{:S(2)}) copy-start(f32[3,128]{1,0:T(4,128)S(1)} %collective-permute-done.2.rest_3_) | copy-start | bytes 4612
